TPU v7x, 512 devices: a whole 4x8x8 slice. The times are simulated.
512 devices in a mesh: pot: 128 (over z_lo, y, x, core), grid: 4 (over z_hi).
Axes of the slice: x: 4, y: 8, z: 8 (z_hi: 4, z_lo: 2; z = z_hi * 2 + z_lo), core: 2. Of those that a mesh axis runs over, the one named last changes fastest.
Arguments:
- potentials: float32 [128, 32, 4096], P('pot', 'grid'), may hold values from -24 to 24
- orbitals: bfloat16 [32, 32, 4096], P(None, 'grid', 'pot'), may hold values from -0.5 to 2
- energies: float32 [32], replicated, may hold values from -2 to -0.2
- local_potential: float32 [32, 4096], replicated, may hold values from 0 to 3
- inverse_factor: bfloat16 [128, 128], replicated, may hold values from -8 to 8, as said below
Outputs:
- updated: float32 [128, 32, 4096], P('pot', 'grid')
- margins: float32 [128, 128], P('pot')
Inputs may be any that keep to these rules, and one draw needn't show every extreme that they name: `inverse_factor`: lower triangular with a positive diagonal.
All inputs are finite; a program needn't handle non-finite values.
Results may differ from a plain program's by a relative error of at most 0.0029.
Values may be sent and summed in bfloat16 or wider, within the bound.
A program may use at most 64 MiB of HBM per device.

v0:
```python
import jax
import jax.numpy as jnp
from jax import lax
from jax.sharding import PartitionSpec as P

NX = 64
NY = 64
NZ = 32
ORBITALS = 32
BLOCKS = 4
SWEEPS = 4
DAMPING = 0.8


def padded_2(block, sides, width):
    for axis, dim in sides:
        count = lax.axis_size(axis)
        forward = [(i, i + 1) for i in range(count - 1)]
        backward = [(target, source) for source, target in forward]
        low = lax.ppermute(
            lax.slice_in_dim(block, block.shape[dim] - width, None, axis=dim), axis, forward
        )
        high = lax.ppermute(lax.slice_in_dim(block, 0, width, axis=dim), axis, backward)
        block = jnp.concatenate([low, block, high], axis=dim)
    return block


def plane_neighbours(field, row_width):
    plane_size = field.shape[-1]
    widths = [(0, 0)] * (field.ndim - 1)
    padded = jnp.pad(field, widths + [(row_width, row_width)])
    along_y = padded[..., 2 * row_width :] + padded[..., :plane_size]
    column = jnp.arange(plane_size, dtype=jnp.int32) % row_width
    padded = jnp.pad(field, widths + [(1, 1)])
    right_side = jnp.where(column == row_width - 1, 0.0, padded[..., 2:])
    left_side = jnp.where(column == 0, 0.0, padded[..., :plane_size])
    return along_y + right_side + left_side


def across_slabs(answer):
    padded = padded_2(answer, (("grid", 2),), 1)
    return padded[:, :, 2:] + padded[:, :, :-2]


def absorb(orbital_block, energy_block, fields, local_here, along_planes):
    orbital = orbital_block.astype(jnp.float32)[:, None]
    diagonal = (3.0 + local_here[None] - energy_block[:, None, None])[:, None]
    source = -orbital * fields[None]
    answer = DAMPING * source / diagonal
    for sweep_index in range(SWEEPS - 1):
        nearby = along_planes(answer) + plane_neighbours(answer, NX)
        answer = answer + DAMPING * (source - diagonal * answer + 0.5 * nearby) / diagonal
    return jnp.sum(orbital * answer, axis=0)


def local(potentials, orbitals, energies, local_potential, inverse_factor):
    slab_depth = potentials.shape[1]
    grid_index = lax.axis_index("grid")
    local_here = lax.dynamic_slice_in_dim(local_potential, grid_index * slab_depth, slab_depth, 0)
    block_size = ORBITALS // BLOCKS
    response = jnp.zeros(potentials.shape, jnp.float32)
    for number in range(BLOCKS):
        orbital_block = orbitals[number * block_size : (number + 1) * block_size]
        gathered = lax.all_gather(orbital_block, "pot", axis=2, tiled=True)
        energy_block = energies[number * block_size : (number + 1) * block_size]
        response = response + absorb(gathered, energy_block, potentials, local_here, across_slabs)
    trial_block = (potentials + 4.0 / ORBITALS * response).astype(jnp.bfloat16)
    by_cells = lax.all_to_all(trial_block, "pot", split_axis=2, concat_axis=0, tiled=True)
    row_count = by_cells.shape[0]
    flattened = by_cells.reshape(row_count, -1)
    partial_margins = lax.dot_general(
        flattened, flattened, (((1,), (1,)), ((), ())), preferred_element_type=jnp.float32
    )
    combined = jnp.dot(inverse_factor, flattened, preferred_element_type=jnp.float32).reshape(
        by_cells.shape
    )
    updated = lax.all_to_all(combined, "pot", split_axis=0, concat_axis=2, tiled=True)
    own_count = potentials.shape[0]
    summed_all = lax.psum(partial_margins, ("pot", "grid"))
    own_rows = lax.dynamic_slice_in_dim(summed_all, lax.axis_index("pot") * own_count, own_count, 0)
    margins = own_rows / (NX * NY * NZ)
    return (updated, margins)


def solution(mesh):
    in_specs = (P("pot", "grid", None), P(None, "grid", "pot"), P(), P(), P())
    out_specs = (P("pot", "grid", None), P("pot", None))
    return jax.shard_map(local, mesh=mesh, in_specs=in_specs, out_specs=out_specs, check_vma=False)
```

profile of v0, /device:TPU:1, one launch (start us, length us, event | category | flops | bytes accessed | tf_op | source)
XLA Modules:
  0.0 1255.0 jit_solution(13859245160564547657)
XLA Ops:
  8.1 192.4 %all_gather.12 = bf16[8,8,4096]{1,0,2:T(8,128)(2,1)} all-gather(bf16[8,8,32]{1,0,2:T(8,128)(2,1)S(1)} %copy.397), channel_id=1, replica_groups=mesh['pot'=128,'grid'=4] {'pot'}, dimensions={2}, use_global_device_ids=true | all-gather | bytes 528384 | tf_op jit(solution)/shard_map/all_gather | solution.py:64
  200.4 7.9 copy.321
  208.4 184.1 %all_gather.13 = bf16[8,8,4096]{1,0,2:T(8,128)(2,1)} all-gather(bf16[8,8,32]{1,0,2:T(8,128)(2,1)S(1)} %copy.398), channel_id=1, replica_groups=mesh['pot'=128,'grid'=4] {'pot'}, dimensions={2}, use_global_device_ids=true | all-gather | bytes 528384 | tf_op jit(solution)/shard_map/all_gather | solution.py:64
  392.5 7.9 copy.338
  400.5 185.2 %all_gather.14 = bf16[8,8,4096]{1,0,2:T(8,128)(2,1)} all-gather(bf16[8,8,32]{1,0,2:T(8,128)(2,1)S(1)} %copy.399), channel_id=1, replica_groups=mesh['pot'=128,'grid'=4] {'pot'}, dimensions={2}, use_global_device_ids=true | all-gather | bytes 528384 | tf_op jit(solution)/shard_map/all_gather | solution.py:64
  585.7 7.9 copy.355
  593.7 184.1 %all_gather.15 = bf16[8,8,4096]{1,0,2:T(8,128)(2,1)} all-gather(bf16[8,8,32]{1,0,2:T(8,128)(2,1)S(1)} %copy.400), channel_id=1, replica_groups=mesh['pot'=128,'grid'=4] {'pot'}, dimensions={2}, use_global_device_ids=true | all-gather | bytes 528384 | tf_op jit(solution)/shard_map/all_gather | solution.py:64
  777.8 7.9 copy.372
  789.7 6.4 collective-permute-start.7
  797.6 6.7 collective-permute-start.1
  806.6 6.1 collective-permute-start.13
  816.3 6.1 collective-permute-start.19
  825.8 6.1 collective-permute-start.9
  835.3 6.1 collective-permute-start.3
  844.9 6.1 collective-permute-start.15
  854.5 6.1 collective-permute-start.21
  860.8 11.6 collective-permute-start.10
  874.5 6.1 collective-permute-start.11
  884.2 6.1 collective-permute-start.5
  894.0 6.1 collective-permute-start.17
  903.1 6.1 collective-permute-start.23
  918.1 22.4 %reduce.4 = bf16[4096,8]{1,0:T(8,128)(2,1)S(1)} reduce(bf16[4096,1,8]{2,1,0:T(2,128)(2,1)S(1)} %bitcast.279, bf16[]{:T(256)} %broadcast.208), dimensions={1}, to_apply=%bitcast.262.reduce_sub_computation | reduce | bytes 131074
  941.6 21.8 %all_to_all.33 = bf16[128,2,128]{2,1,0:T(2,128)(2,1)S(1)} all-to-all(bf16[128,2,128]{2,1,0:T(2,128)(2,1)S(1)} %reshape.105), channel_id=1, replica_groups=mesh['pot'=128,'grid'=4] {'pot'}, dimensions={0} | all-to-all | bytes 131072 | tf_op jit(solution)/shard_map/all_to_all | solution.py:68
  976.4 267.5 %all-reduce.26.cloned.1.call-done = f32[128,128]{1,0:T(8,128)} async-done(((f32[128,128]{1,0:T(8,128)}), f32[128,128]{1,0:T(8,128)}) %all-reduce.26.cloned.1.call-update) | async-done | bytes 65552 | tf_op jit(solution)/shard_map/psum | solution.py:79
  (142 shorter events, 64.8 us)
Async XLA Ops:
  788.3 18.2 %collective-permute-start.6 = (f32[8,1,1,4096]{3,0,2,1:T(8,128)S(1)}, f32[8,1,1,4096]{3,0,2,1:T(8,128)S(1)}, u32[]{:S(2)}, u32[]{:S(2)}) collective-permute-start(f32[8,1,1,4096]{3,0,2,1:T(8,128)S(1)} %copy.339), channel_id=1, source_target_pairs={{1,0},{2,1},{3,2},{5,4},{6,5},{7,6},{9,8},{10,9},{11,10},{13,12},{... | collective-permute-start | bytes 393224 | tf_op jit(solution)/shard_map/ppermute | solution.py:23
  789.7 23.1 %collective-permute-start.7 = (f32[8,1,1,4096]{3,0,2,1:T(8,128)S(1)}, f32[8,1,1,4096]{3,0,2,1:T(8,128)S(1)}, u32[]{:S(2)}, u32[]{:S(2)}) collective-permute-start(f32[8,1,1,4096]{3,0,2,1:T(8,128)S(1)} %copy.341), channel_id=1, source_target_pairs={{0,1},{1,2},{2,3},{4,5},{5,6},{6,7},{8,9},{9,10},{10,11},{12,13},{... | collective-permute-start | bytes 393224 | tf_op jit(solution)/shard_map/ppermute | solution.py:20
  796.3 20.0 %collective-permute-start = (f32[8,1,1,4096]{3,0,2,1:T(8,128)S(1)}, f32[8,1,1,4096]{3,0,2,1:T(8,128)S(1)}, u32[]{:S(2)}, u32[]{:S(2)}) collective-permute-start(f32[8,1,1,4096]{3,0,2,1:T(8,128)S(1)} %copy.322), channel_id=1, source_target_pairs={{1,0},{2,1},{3,2},{5,4},{6,5},{7,6},{9,8},{10,9},{11,10},{13,12},{... | collective-permute-start | bytes 393224 | tf_op jit(solution)/shard_map/ppermute | solution.py:23
  797.6 24.9 %collective-permute-start.1 = (f32[8,1,1,4096]{3,0,2,1:T(8,128)S(1)}, f32[8,1,1,4096]{3,0,2,1:T(8,128)S(1)}, u32[]{:S(2)}, u32[]{:S(2)}) collective-permute-start(f32[8,1,1,4096]{3,0,2,1:T(8,128)S(1)} %copy.324), channel_id=1, source_target_pairs={{0,1},{1,2},{2,3},{4,5},{5,6},{6,7},{8,9},{9,10},{10,11},{12,13},{... | collective-permute-start | bytes 393224 | tf_op jit(solution)/shard_map/ppermute | solution.py:20
  805.0 20.8 %collective-permute-start.12 = (f32[8,1,1,4096]{3,0,2,1:T(8,128)S(1)}, f32[8,1,1,4096]{3,0,2,1:T(8,128)S(1)}, u32[]{:S(2)}, u32[]{:S(2)}) collective-permute-start(f32[8,1,1,4096]{3,0,2,1:T(8,128)S(1)} %copy.356), channel_id=1, source_target_pairs={{1,0},{2,1},{3,2},{5,4},{6,5},{7,6},{9,8},{10,9},{11,10},{13,12},{... | collective-permute-start | bytes 393224 | tf_op jit(solution)/shard_map/ppermute | solution.py:23
  806.6 25.4 %collective-permute-start.13 = (f32[8,1,1,4096]{3,0,2,1:T(8,128)S(1)}, f32[8,1,1,4096]{3,0,2,1:T(8,128)S(1)}, u32[]{:S(2)}, u32[]{:S(2)}) collective-permute-start(f32[8,1,1,4096]{3,0,2,1:T(8,128)S(1)} %copy.358), channel_id=1, source_target_pairs={{0,1},{1,2},{2,3},{4,5},{5,6},{6,7},{8,9},{9,10},{10,11},{12,13},{... | collective-permute-start | bytes 393224 | tf_op jit(solution)/shard_map/ppermute | solution.py:20
  812.8 22.4 %collective-permute-start.18 = (f32[8,1,1,4096]{3,0,2,1:T(8,128)S(1)}, f32[8,1,1,4096]{3,0,2,1:T(8,128)S(1)}, u32[]{:S(2)}, u32[]{:S(2)}) collective-permute-start(f32[8,1,1,4096]{3,0,2,1:T(8,128)S(1)} %copy.373), channel_id=1, source_target_pairs={{1,0},{2,1},{3,2},{5,4},{6,5},{7,6},{9,8},{10,9},{11,10},{13,12},{... | collective-permute-start | bytes 393224 | tf_op jit(solution)/shard_map/ppermute | solution.py:23
  816.3 25.3 %collective-permute-start.19 = (f32[8,1,1,4096]{3,0,2,1:T(8,128)S(1)}, f32[8,1,1,4096]{3,0,2,1:T(8,128)S(1)}, u32[]{:S(2)}, u32[]{:S(2)}) collective-permute-start(f32[8,1,1,4096]{3,0,2,1:T(8,128)S(1)} %copy.375), channel_id=1, source_target_pairs={{0,1},{1,2},{2,3},{4,5},{5,6},{6,7},{8,9},{9,10},{10,11},{12,13},{... | collective-permute-start | bytes 393224 | tf_op jit(solution)/shard_map/ppermute | solution.py:20
  822.5 22.3 %collective-permute-start.8 = (f32[8,1,1,4096]{3,0,2,1:T(8,128)S(1)}, f32[8,1,1,4096]{3,0,2,1:T(8,128)S(1)}, u32[]{:S(2)}, u32[]{:S(2)}) collective-permute-start(f32[8,1,1,4096]{3,0,2,1:T(8,128)S(1)} %copy.344), channel_id=1, source_target_pairs={{1,0},{2,1},{3,2},{5,4},{6,5},{7,6},{9,8},{10,9},{11,10},{13,12},{... | collective-permute-start | bytes 393224 | tf_op jit(solution)/shard_map/ppermute | solution.py:23
  825.8 25.4 %collective-permute-start.9 = (f32[8,1,1,4096]{3,0,2,1:T(8,128)S(1)}, f32[8,1,1,4096]{3,0,2,1:T(8,128)S(1)}, u32[]{:S(2)}, u32[]{:S(2)}) collective-permute-start(f32[8,1,1,4096]{3,0,2,1:T(8,128)S(1)} %copy.346), channel_id=1, source_target_pairs={{0,1},{1,2},{2,3},{4,5},{5,6},{6,7},{8,9},{9,10},{10,11},{12,13},{... | collective-permute-start | bytes 393224 | tf_op jit(solution)/shard_map/ppermute | solution.py:20
  832.0 22.5 %collective-permute-start.2 = (f32[8,1,1,4096]{3,0,2,1:T(8,128)S(1)}, f32[8,1,1,4096]{3,0,2,1:T(8,128)S(1)}, u32[]{:S(2)}, u32[]{:S(2)}) collective-permute-start(f32[8,1,1,4096]{3,0,2,1:T(8,128)S(1)} %copy.327), channel_id=1, source_target_pairs={{1,0},{2,1},{3,2},{5,4},{6,5},{7,6},{9,8},{10,9},{11,10},{13,12},{... | collective-permute-start | bytes 393224 | tf_op jit(solution)/shard_map/ppermute | solution.py:23
  835.3 25.5 %collective-permute-start.3 = (f32[8,1,1,4096]{3,0,2,1:T(8,128)S(1)}, f32[8,1,1,4096]{3,0,2,1:T(8,128)S(1)}, u32[]{:S(2)}, u32[]{:S(2)}) collective-permute-start(f32[8,1,1,4096]{3,0,2,1:T(8,128)S(1)} %copy.329), channel_id=1, source_target_pairs={{0,1},{1,2},{2,3},{4,5},{5,6},{6,7},{8,9},{9,10},{10,11},{12,13},{... | collective-permute-start | bytes 393224 | tf_op jit(solution)/shard_map/ppermute | solution.py:20
  841.5 32.9 %collective-permute-start.14 = (f32[8,1,1,4096]{3,0,2,1:T(8,128)S(1)}, f32[8,1,1,4096]{3,0,2,1:T(8,128)S(1)}, u32[]{:S(2)}, u32[]{:S(2)}) collective-permute-start(f32[8,1,1,4096]{3,0,2,1:T(8,128)S(1)} %copy.361), channel_id=1, source_target_pairs={{1,0},{2,1},{3,2},{5,4},{6,5},{7,6},{9,8},{10,9},{11,10},{13,12},{... | collective-permute-start | bytes 393224 | tf_op jit(solution)/shard_map/ppermute | solution.py:23
  844.9 35.9 %collective-permute-start.15 = (f32[8,1,1,4096]{3,0,2,1:T(8,128)S(1)}, f32[8,1,1,4096]{3,0,2,1:T(8,128)S(1)}, u32[]{:S(2)}, u32[]{:S(2)}) collective-permute-start(f32[8,1,1,4096]{3,0,2,1:T(8,128)S(1)} %copy.363), channel_id=1, source_target_pairs={{0,1},{1,2},{2,3},{4,5},{5,6},{6,7},{8,9},{9,10},{10,11},{12,13},{... | collective-permute-start | bytes 393224 | tf_op jit(solution)/shard_map/ppermute | solution.py:20
  851.1 33.0 %collective-permute-start.20 = (f32[8,1,1,4096]{3,0,2,1:T(8,128)S(1)}, f32[8,1,1,4096]{3,0,2,1:T(8,128)S(1)}, u32[]{:S(2)}, u32[]{:S(2)}) collective-permute-start(f32[8,1,1,4096]{3,0,2,1:T(8,128)S(1)} %copy.378), channel_id=1, source_target_pairs={{1,0},{2,1},{3,2},{5,4},{6,5},{7,6},{9,8},{10,9},{11,10},{13,12},{... | collective-permute-start | bytes 393224 | tf_op jit(solution)/shard_map/ppermute | solution.py:23
  854.5 35.9 %collective-permute-start.21 = (f32[8,1,1,4096]{3,0,2,1:T(8,128)S(1)}, f32[8,1,1,4096]{3,0,2,1:T(8,128)S(1)}, u32[]{:S(2)}, u32[]{:S(2)}) collective-permute-start(f32[8,1,1,4096]{3,0,2,1:T(8,128)S(1)} %copy.380), channel_id=1, source_target_pairs={{0,1},{1,2},{2,3},{4,5},{5,6},{6,7},{8,9},{9,10},{10,11},{12,13},{... | collective-permute-start | bytes 393224 | tf_op jit(solution)/shard_map/ppermute | solution.py:20
  860.8 33.2 %collective-permute-start.10 = (f32[8,1,1,4096]{3,0,2,1:T(8,128)S(1)}, f32[8,1,1,4096]{3,0,2,1:T(8,128)S(1)}, u32[]{:S(2)}, u32[]{:S(2)}) collective-permute-start(f32[8,1,1,4096]{3,0,2,1:T(8,128)S(1)} %copy.349), channel_id=1, source_target_pairs={{1,0},{2,1},{3,2},{5,4},{6,5},{7,6},{9,8},{10,9},{11,10},{13,12},{... | collective-permute-start | bytes 393224 | tf_op jit(solution)/shard_map/ppermute | solution.py:23
  874.5 25.7 %collective-permute-start.11 = (f32[8,1,1,4096]{3,0,2,1:T(8,128)S(1)}, f32[8,1,1,4096]{3,0,2,1:T(8,128)S(1)}, u32[]{:S(2)}, u32[]{:S(2)}) collective-permute-start(f32[8,1,1,4096]{3,0,2,1:T(8,128)S(1)} %copy.351), channel_id=1, source_target_pairs={{0,1},{1,2},{2,3},{4,5},{5,6},{6,7},{8,9},{9,10},{10,11},{12,13},{... | collective-permute-start | bytes 393224 | tf_op jit(solution)/shard_map/ppermute | solution.py:20
  880.7 22.4 %collective-permute-start.4 = (f32[8,1,1,4096]{3,0,2,1:T(8,128)S(1)}, f32[8,1,1,4096]{3,0,2,1:T(8,128)S(1)}, u32[]{:S(2)}, u32[]{:S(2)}) collective-permute-start(f32[8,1,1,4096]{3,0,2,1:T(8,128)S(1)} %copy.332), channel_id=1, source_target_pairs={{1,0},{2,1},{3,2},{5,4},{6,5},{7,6},{9,8},{10,9},{11,10},{13,12},{... | collective-permute-start | bytes 393224 | tf_op jit(solution)/shard_map/ppermute | solution.py:23
  884.2 25.2 %collective-permute-start.5 = (f32[8,1,1,4096]{3,0,2,1:T(8,128)S(1)}, f32[8,1,1,4096]{3,0,2,1:T(8,128)S(1)}, u32[]{:S(2)}, u32[]{:S(2)}) collective-permute-start(f32[8,1,1,4096]{3,0,2,1:T(8,128)S(1)} %copy.334), channel_id=1, source_target_pairs={{0,1},{1,2},{2,3},{4,5},{5,6},{6,7},{8,9},{9,10},{10,11},{12,13},{... | collective-permute-start | bytes 393224 | tf_op jit(solution)/shard_map/ppermute | solution.py:20
  890.4 20.6 %collective-permute-start.16 = (f32[8,1,1,4096]{3,0,2,1:T(8,128)S(1)}, f32[8,1,1,4096]{3,0,2,1:T(8,128)S(1)}, u32[]{:S(2)}, u32[]{:S(2)}) collective-permute-start(f32[8,1,1,4096]{3,0,2,1:T(8,128)S(1)} %copy.366), channel_id=1, source_target_pairs={{1,0},{2,1},{3,2},{5,4},{6,5},{7,6},{9,8},{10,9},{11,10},{13,12},{... | collective-permute-start | bytes 393224 | tf_op jit(solution)/shard_map/ppermute | solution.py:23
  894.0 17.2 %collective-permute-start.17 = (f32[8,1,1,4096]{3,0,2,1:T(8,128)S(1)}, f32[8,1,1,4096]{3,0,2,1:T(8,128)S(1)}, u32[]{:S(2)}, u32[]{:S(2)}) collective-permute-start(f32[8,1,1,4096]{3,0,2,1:T(8,128)S(1)} %copy.368), channel_id=1, source_target_pairs={{0,1},{1,2},{2,3},{4,5},{5,6},{6,7},{8,9},{9,10},{10,11},{12,13},{... | collective-permute-start | bytes 393224 | tf_op jit(solution)/shard_map/ppermute | solution.py:20
  969.7 275.5 %all-to-all-start.1 = ((f32[128,1,256]{2,1,0:T(1,128)}), f32[128,1,256]{2,1,0:T(1,128)S(1)}, u32[]{:S(2)}, u32[]{:S(2)}) async-start(f32[128,1,256]{2,1,0:T(1,128)} %reshape.107), calls=%async_computation.1 | async-start | bytes 262144 | tf_op jit(solution)/shard_map/all_to_all | solution.py:77
  975.5 268.4 %all-reduce.26.cloned.1.call-start = ((), (), s32[]{:S(2)}) async-start(), calls=%async_computation.2 | async-start | bytes 131072 | tf_op jit(solution)/shard_map/psum | solution.py:79
  (5 other events, 1000.4 us)
Sparse Core Ops, SparseCore 0:
  981.3 262.5 all-reduce.25
where the time goes:
time: 1260 us; the launch traced here: 1250 us
  blocking collectives  768 us (61%)
  waiting for transfers between devices  268 us (21%)
  starting transfers between devices  106 us (8%)
  local copies, waits for them, and re-layouts  52.8 us (4%)
  other arithmetic  44.6 us (4%)
  between operations  15.4 us (1%)
    all_gather x4, blocking collectives, local(): gathered = lax.all_gather(orbital_block, 'pot', axis=2, tiled=True)  746 us
    psum x1, waiting for transfers between devices, local(): summed_all = lax.psum(partial_margins, ('pot', 'grid'))  268 us
    ppermute x12, starting transfers between devices, padded_2(): lax.ppermute(lax.slice_in_dim(block, block.shape[dim] - width, None, axis...  74.2 us
    all_gather x4, local copies, waits for them, and re-layouts, local(): gathered = lax.all_gather(orbital_block, 'pot', axis=2, tiled=True)  31.5 us
    ppermute x12, starting transfers between devices, padded_2(): lax.ppermute(lax.slice_in_dim(block, 0, width, axis=dim), axis, backward)  26 us
  transfers between devices with their start and end apart: 26, of which 1 were waited for; matrix products, arithmetic and copies ran while one was open for 2% of the time, Pallas kernels for 0%

commit v1 on v0

--- a/solution.py
+++ b/solution.py
@@ -76,7 +76,7 @@
     )
     updated = lax.all_to_all(combined, "pot", split_axis=0, concat_axis=2, tiled=True)
     own_count = potentials.shape[0]
-    summed_all = lax.psum(partial_margins, ("pot", "grid"))
+    summed_all = jnp.sum(lax.all_gather(partial_margins, ("pot", "grid")), axis=0)
     own_rows = lax.dynamic_slice_in_dim(summed_all, lax.axis_index("pot") * own_count, own_count, 0)
     margins = own_rows / (NX * NY * NZ)
     return (updated, margins)

time: 1260 us -> 2460 us (1.95)
  waiting for transfers between devices: 268 us -> 1450 us
    all_gather x0 -> x1, waiting for transfers between devices: none -> 1430 us  [local(): lax.all_gather(partial_margins, ('pot', 'grid'))]
    psum x1 -> x0, waiting for transfers between devices: 268 us -> none  [local(): summed_all = lax.psum(partial_margins, ('pot', 'grid'))]
  transfers between devices with their start and end apart: 26 -> 26, of which waited for: 1 -> 4; matrix products, arithmetic and copies ran while one was open for 2% -> 1% of each run, Pallas kernels for 0% -> 0%
where the time goes in v1:
time: 2460 us; the launch traced here: 2450 us
  waiting for transfers between devices  1450 us (59%)
  blocking collectives  768 us (31%)
  starting transfers between devices  100 us (4%)
  other arithmetic  57 us (2%)
  local copies, waits for them, and re-layouts  53.7 us (2%)
    all_gather x1, waiting for transfers between devices, local(): lax.all_gather(partial_margins, ('pot', 'grid'))  1430 us
    all_gather x4, blocking collectives, local(): gathered = lax.all_gather(orbital_block, 'pot', axis=2, tiled=True)  746 us
    ppermute x12, starting transfers between devices, padded_2(): lax.ppermute(lax.slice_in_dim(block, block.shape[dim] - width, None, axis...  79 us
  transfers between devices with their start and end apart: 26, of which 4 were waited for; matrix products, arithmetic and copies ran while one was open for 1% of the time, Pallas kernels for 0%

profile of v1, /device:TPU:1, one launch (start us, length us, event | category | flops | bytes accessed | tf_op | source)
XLA Modules:
  0.0 2447.0 jit_solution(2299360249630387679)
XLA Ops:
  9.3 192.4 %all_gather.21 = bf16[8,8,4096]{1,0,2:T(8,128)(2,1)} all-gather(bf16[8,8,32]{1,0,2:T(8,128)(2,1)S(1)} %copy.400), channel_id=1, replica_groups=mesh['pot'=128,'grid'=4] {'pot'}, dimensions={2}, use_global_device_ids=true | all-gather | bytes 528384 | tf_op jit(solution)/shard_map/all_gather | solution.py:64
  201.7 7.9 copy.372
  209.6 184.1 %all_gather.18 = bf16[8,8,4096]{1,0,2:T(8,128)(2,1)} all-gather(bf16[8,8,32]{1,0,2:T(8,128)(2,1)S(1)} %copy.397), channel_id=1, replica_groups=mesh['pot'=128,'grid'=4] {'pot'}, dimensions={2}, use_global_device_ids=true | all-gather | bytes 528384 | tf_op jit(solution)/shard_map/all_gather | solution.py:64
  393.7 7.9 copy.321
  401.5 185.2 %all_gather.20 = bf16[8,8,4096]{1,0,2:T(8,128)(2,1)} all-gather(bf16[8,8,32]{1,0,2:T(8,128)(2,1)S(1)} %copy.399), channel_id=1, replica_groups=mesh['pot'=128,'grid'=4] {'pot'}, dimensions={2}, use_global_device_ids=true | all-gather | bytes 528384 | tf_op jit(solution)/shard_map/all_gather | solution.py:64
  586.8 7.9 copy.355
  594.6 184.1 %all_gather.19 = bf16[8,8,4096]{1,0,2:T(8,128)(2,1)} all-gather(bf16[8,8,32]{1,0,2:T(8,128)(2,1)S(1)} %copy.398), channel_id=1, replica_groups=mesh['pot'=128,'grid'=4] {'pot'}, dimensions={2}, use_global_device_ids=true | all-gather | bytes 528384 | tf_op jit(solution)/shard_map/all_gather | solution.py:64
  778.7 7.9 copy.338
  790.5 6.4 collective-permute-start.1
  797.1 6.1 collective-permute-start.7
  806.8 5.5 collective-permute-start.19
  831.0 6.1 collective-permute-start.3
  840.5 6.1 collective-permute-start.15
  850.0 6.1 collective-permute-start.21
  859.8 16.3 collective-permute-start.11
  879.7 6.1 collective-permute-start.5
  889.4 6.1 collective-permute-start.17
  899.1 6.1 collective-permute-start.23
  920.8 22.4 reduce.4
  944.3 22.7 all_to_all.33
  974.1 5.8 all-to-all-start.1
  980.0 12.5 all-to-all-done.1
  995.1 1431.0 %all-gather.3.cloned.1.call-done = f32[65536,128]{1,0:T(8,128)} async-done(((f32[128,128]{1,0:T(8,128)}), f32[65536,128]{1,0:T(8,128)}) %all-gather.3.cloned.1.call-update) | async-done | bytes 33554448 | tf_op jit(solution)/shard_map/all_gather | solution.py:79
  2426.2 13.1 reduce_sum.49
  (141 shorter events, 75.8 us)
Async XLA Ops:
  7.2 2419.0 %all-gather.3.cloned.1.call-start = ((), (), s32[]{:S(2)}) async-start(), calls=%async_computation.2 | async-start | bytes 33619968 | tf_op jit(solution)/shard_map/all_gather | solution.py:79
  789.2 31.5 %collective-permute-start = (f32[8,1,1,4096]{3,0,2,1:T(8,128)S(1)}, f32[8,1,1,4096]{3,0,2,1:T(8,128)S(1)}, u32[]{:S(2)}, u32[]{:S(2)}) collective-permute-start(f32[8,1,1,4096]{3,0,2,1:T(8,128)S(1)} %copy.322), channel_id=1, source_target_pairs={{1,0},{2,1},{3,2},{5,4},{6,5},{7,6},{9,8},{10,9},{11,10},{13,12},{... | collective-permute-start | bytes 393224 | tf_op jit(solution)/shard_map/ppermute | solution.py:23
  790.5 31.6 %collective-permute-start.1 = (f32[8,1,1,4096]{3,0,2,1:T(8,128)S(1)}, f32[8,1,1,4096]{3,0,2,1:T(8,128)S(1)}, u32[]{:S(2)}, u32[]{:S(2)}) collective-permute-start(f32[8,1,1,4096]{3,0,2,1:T(8,128)S(1)} %copy.324), channel_id=1, source_target_pairs={{0,1},{1,2},{2,3},{4,5},{5,6},{6,7},{8,9},{9,10},{10,11},{12,13},{... | collective-permute-start | bytes 393224 | tf_op jit(solution)/shard_map/ppermute | solution.py:20
  803.3 12.9 collective-permute-start.6
  805.2 33.9 %collective-permute-start.18 = (f32[8,1,1,4096]{3,0,2,1:T(8,128)S(1)}, f32[8,1,1,4096]{3,0,2,1:T(8,128)S(1)}, u32[]{:S(2)}, u32[]{:S(2)}) collective-permute-start(f32[8,1,1,4096]{3,0,2,1:T(8,128)S(1)} %copy.373), channel_id=1, source_target_pairs={{1,0},{2,1},{3,2},{5,4},{6,5},{7,6},{9,8},{10,9},{11,10},{13,12},{... | collective-permute-start | bytes 393224 | tf_op jit(solution)/shard_map/ppermute | solution.py:23
  806.8 33.8 %collective-permute-start.19 = (f32[8,1,1,4096]{3,0,2,1:T(8,128)S(1)}, f32[8,1,1,4096]{3,0,2,1:T(8,128)S(1)}, u32[]{:S(2)}, u32[]{:S(2)}) collective-permute-start(f32[8,1,1,4096]{3,0,2,1:T(8,128)S(1)} %copy.375), channel_id=1, source_target_pairs={{0,1},{1,2},{2,3},{4,5},{5,6},{6,7},{8,9},{9,10},{10,11},{12,13},{... | collective-permute-start | bytes 393224 | tf_op jit(solution)/shard_map/ppermute | solution.py:20
  816.2 13.3 collective-permute-start.13
  820.7 10.3 collective-permute-start.12
  822.1 26.5 %collective-permute-start.9 = (f32[8,1,1,4096]{3,0,2,1:T(8,128)S(1)}, f32[8,1,1,4096]{3,0,2,1:T(8,128)S(1)}, u32[]{:S(2)}, u32[]{:S(2)}) collective-permute-start(f32[8,1,1,4096]{3,0,2,1:T(8,128)S(1)} %copy.346), channel_id=1, source_target_pairs={{0,1},{1,2},{2,3},{4,5},{5,6},{6,7},{8,9},{9,10},{10,11},{12,13},{... | collective-permute-start | bytes 393224 | tf_op jit(solution)/shard_map/ppermute | solution.py:20
  829.6 20.5 collective-permute-start.8
  831.0 27.3 %collective-permute-start.3 = (f32[8,1,1,4096]{3,0,2,1:T(8,128)S(1)}, f32[8,1,1,4096]{3,0,2,1:T(8,128)S(1)}, u32[]{:S(2)}, u32[]{:S(2)}) collective-permute-start(f32[8,1,1,4096]{3,0,2,1:T(8,128)S(1)} %copy.329), channel_id=1, source_target_pairs={{0,1},{1,2},{2,3},{4,5},{5,6},{6,7},{8,9},{9,10},{10,11},{12,13},{... | collective-permute-start | bytes 393224 | tf_op jit(solution)/shard_map/ppermute | solution.py:20
  839.1 20.7 collective-permute-start.2
  840.5 37.7 %collective-permute-start.15 = (f32[8,1,1,4096]{3,0,2,1:T(8,128)S(1)}, f32[8,1,1,4096]{3,0,2,1:T(8,128)S(1)}, u32[]{:S(2)}, u32[]{:S(2)}) collective-permute-start(f32[8,1,1,4096]{3,0,2,1:T(8,128)S(1)} %copy.363), channel_id=1, source_target_pairs={{0,1},{1,2},{2,3},{4,5},{5,6},{6,7},{8,9},{9,10},{10,11},{12,13},{... | collective-permute-start | bytes 393224 | tf_op jit(solution)/shard_map/ppermute | solution.py:20
  848.6 31.1 %collective-permute-start.14 = (f32[8,1,1,4096]{3,0,2,1:T(8,128)S(1)}, f32[8,1,1,4096]{3,0,2,1:T(8,128)S(1)}, u32[]{:S(2)}, u32[]{:S(2)}) collective-permute-start(f32[8,1,1,4096]{3,0,2,1:T(8,128)S(1)} %copy.361), channel_id=1, source_target_pairs={{1,0},{2,1},{3,2},{5,4},{6,5},{7,6},{9,8},{10,9},{11,10},{13,12},{... | collective-permute-start | bytes 393224 | tf_op jit(solution)/shard_map/ppermute | solution.py:23
  850.0 37.9 %collective-permute-start.21 = (f32[8,1,1,4096]{3,0,2,1:T(8,128)S(1)}, f32[8,1,1,4096]{3,0,2,1:T(8,128)S(1)}, u32[]{:S(2)}, u32[]{:S(2)}) collective-permute-start(f32[8,1,1,4096]{3,0,2,1:T(8,128)S(1)} %copy.380), channel_id=1, source_target_pairs={{0,1},{1,2},{2,3},{4,5},{5,6},{6,7},{8,9},{9,10},{10,11},{12,13},{... | collective-permute-start | bytes 393224 | tf_op jit(solution)/shard_map/ppermute | solution.py:20
  858.3 31.1 %collective-permute-start.20 = (f32[8,1,1,4096]{3,0,2,1:T(8,128)S(1)}, f32[8,1,1,4096]{3,0,2,1:T(8,128)S(1)}, u32[]{:S(2)}, u32[]{:S(2)}) collective-permute-start(f32[8,1,1,4096]{3,0,2,1:T(8,128)S(1)} %copy.378), channel_id=1, source_target_pairs={{1,0},{2,1},{3,2},{5,4},{6,5},{7,6},{9,8},{10,9},{11,10},{13,12},{... | collective-permute-start | bytes 393224 | tf_op jit(solution)/shard_map/ppermute | solution.py:23
  859.8 37.9 %collective-permute-start.11 = (f32[8,1,1,4096]{3,0,2,1:T(8,128)S(1)}, f32[8,1,1,4096]{3,0,2,1:T(8,128)S(1)}, u32[]{:S(2)}, u32[]{:S(2)}) collective-permute-start(f32[8,1,1,4096]{3,0,2,1:T(8,128)S(1)} %copy.351), channel_id=1, source_target_pairs={{0,1},{1,2},{2,3},{4,5},{5,6},{6,7},{8,9},{9,10},{10,11},{12,13},{... | collective-permute-start | bytes 393224 | tf_op jit(solution)/shard_map/ppermute | solution.py:20
  878.2 20.9 collective-permute-start.10
  879.7 27.2 %collective-permute-start.5 = (f32[8,1,1,4096]{3,0,2,1:T(8,128)S(1)}, f32[8,1,1,4096]{3,0,2,1:T(8,128)S(1)}, u32[]{:S(2)}, u32[]{:S(2)}) collective-permute-start(f32[8,1,1,4096]{3,0,2,1:T(8,128)S(1)} %copy.334), channel_id=1, source_target_pairs={{0,1},{1,2},{2,3},{4,5},{5,6},{6,7},{8,9},{9,10},{10,11},{12,13},{... | collective-permute-start | bytes 393224 | tf_op jit(solution)/shard_map/ppermute | solution.py:20
  888.0 20.3 collective-permute-start.4
  889.4 20.5 collective-permute-start.17
  897.7 12.4 collective-permute-start.16
  899.1 12.6 collective-permute-start.23
  974.1 18.4 all-to-all-start.1
  (4 other events, 992.9 us)
Sparse Core Ops, SparseCore 0:
  972.9 1453.2 all-gather.2
